TPU v7x, 32 devices: a whole 2x2x4 slice. The times are simulated.
32 devices in a mesh: tm: 2 (over core), height: 16 (over z, y, x).
Axes of the slice: x: 2, y: 2, z: 4, core: 2. Of those that a mesh axis runs over, the one named last changes fastest.
Arguments:
- queries: bfloat16 [8, 16, 32, 2560], P('tm', 'height'), may hold values from -8 to 8
- keys: bfloat16 [8, 16, 32, 2560], P('tm', 'height'), may hold values from -8 to 8
- values: bfloat16 [8, 16, 32, 2560], P('tm', 'height'), may hold values from -6 to 6
- window_mask: int32 [8, 16, 4, 27], P('tm', 'height'), may hold values from 0 to 1, as said below
- pos_t: int32 [8], P('tm'), may hold values from 0 to 127, as said below
- pos_h: int32 [16], P('height'), may hold values from 0 to 31, as said below
- pos_w: int32 [32], replicated, may hold values from 0 to 63, as said below
Outputs:
- attended: bfloat16 [8, 16, 32, 2560], P('tm', 'height')
Inputs may be any that keep to these rules, and one draw needn't show every extreme that they name: `window_mask`: entry (dt+1)*9 + (dr+1)*3 + (db+1) refers to the tile offset by dt frames, dr rows and db tiles along the row; it is 0 wherever that tile lies outside the grid, and the centre entry 13 is always 1. `pos_t`: strictly increasing. `pos_h`: strictly increasing. `pos_w`: strictly increasing.
All inputs are finite; a program needn't handle non-finite values.
Results may differ from a plain program's by a relative error of at most 0.0044.
The roundings to bfloat16 on the way count: a program that leaves them out, or rounds other values in their place, can miss the bound.
Values may be sent and summed in bfloat16 or wider, within the bound.
A program may use at most 128 MiB of HBM per device.

v0:
```python
import functools
import math

import jax
import jax.numpy as jnp
import numpy as np
from jax import lax
from jax.experimental import pallas as pl
from jax.experimental.pallas import tpu as pltpu
from jax.sharding import PartitionSpec as P

HEADS = 20
HEAD_DIM = 128
TILE_W = 8
MESH = pl.DeviceIdType.MESH
NEAR = [(dc, dg) for dc in (-1, 0, 1) for dg in (-1, 0, 1) if (dc, dg) != (0, 0)]


def rope_tables(pos_t, pos_h, pos_w, half_dim):
    pairs_hw = 2 * half_dim // 6
    pairs_time = half_dim - 2 * pairs_hw
    pair_index = jnp.arange(half_dim).astype(jnp.float32)
    freq_time = jnp.where(
        pair_index < pairs_time, jnp.power(10000.0, -pair_index / pairs_time), 0.0
    )
    in_rows = (pair_index >= pairs_time) & (pair_index < pairs_time + pairs_hw)
    freq_rows = jnp.where(in_rows, jnp.power(10000.0, -(pair_index - pairs_time) / pairs_hw), 0.0)
    freq_cols = jnp.where(
        pair_index >= pairs_time + pairs_hw,
        jnp.power(10000.0, -(pair_index - pairs_time - pairs_hw) / pairs_hw),
        0.0,
    )
    angles = (
        pos_t.astype(jnp.float32)[:, None, None, None] * freq_time
        + pos_h.astype(jnp.float32)[None, :, None, None] * freq_rows
        + pos_w.astype(jnp.float32)[None, None, :, None] * freq_cols
    )
    cos_tab = jnp.cos(angles)
    sine_tab = jnp.sin(angles)
    return (jnp.concatenate([cos_tab, cos_tab], -1), jnp.concatenate([-sine_tab, sine_tab], -1))


def mask_selectors(group, width, lanes):
    blocks = width // TILE_W
    slot = lanes // blocks
    keys = 3 * (group + 2) * width
    own = (np.arange(width)[:, None] // TILE_W == np.arange(lanes)[None, :] // slot)
    key = np.arange(keys)
    step_t = key // ((group + 2) * width)
    key_row = key // width % (group + 2)
    key_block = key % width // TILE_W
    pick = np.zeros((group, lanes, keys), np.float32)
    for row in range(group):
        for block in range(blocks):
            step_h = key_row - row
            step_w = key_block - block + 1
            inside = (step_h >= 0) & (step_h < 3) & (step_w >= 0) & (step_w < 3)
            offset = step_t * 9 + step_h * 3 + step_w
            pick[row, (block * slot + offset)[inside], key[inside]] = 1.0
    return own.astype(np.float32), pick


def kernel(
    sizes, q_ref, k_ref, v_ref, cos_ref, sin_ref, mask_ref, own_ref, pick_ref, out_ref,
    rot, ext, first, held, masks, bias,
    a_send, a_recv, n_send, n_recv, f_send, f_recv, t_send, t_recv, o_send, o_recv, m_send, m_recv,
):
    group, groups, parts, frames, width, heads = sizes
    dim = HEAD_DIM
    tokens = group * width
    c = lax.axis_index("tm")
    at = lax.axis_index("height")
    g = at // group
    m = at % group

    def peer(step):
        return (m + step) % group

    def send_rows(j, step):
        to = peer(step)
        return pltpu.make_async_remote_copy(
            src_ref=rot.at[to * heads + j],
            dst_ref=ext.at[j, :, pl.ds(1, frames), m + 1],
            send_sem=a_send.at[j, step - 1],
            recv_sem=a_recv.at[j, m],
            device_id=(c, g * group + to),
            device_id_type=MESH,
        )

    def got_rows(j, step):
        come = peer(step)
        return pltpu.make_async_remote_copy(
            src_ref=rot.at[come * heads + j],
            dst_ref=ext.at[j, :, pl.ds(1, frames), come + 1],
            send_sem=a_send.at[j, step - 1],
            recv_sem=a_recv.at[j, come],
            device_id=(c, g * group + come),
            device_id_type=MESH,
        )

    def near_copy(j, n):
        dc, dg = NEAR[n]
        src_t = {-1: pl.ds(1, 1), 0: pl.ds(1, frames), 1: pl.ds(frames, 1)}[dc]
        dst_t = {-1: pl.ds(frames + 1, 1), 0: pl.ds(1, frames), 1: pl.ds(0, 1)}[dc]
        src_h = {-1: pl.ds(1, 1), 0: pl.ds(1, group), 1: pl.ds(group, 1)}[dg]
        dst_h = {-1: pl.ds(group + 1, 1), 0: pl.ds(1, group), 1: pl.ds(0, 1)}[dg]
        return pltpu.make_async_remote_copy(
            src_ref=ext.at[j, pl.ds(1, 2), src_t, src_h],
            dst_ref=ext.at[j, pl.ds(1, 2), dst_t, dst_h],
            send_sem=n_send.at[j, n],
            recv_sem=n_recv.at[j, n],
            device_id=(c + dc, at + dg * group),
            device_id_type=MESH,
        )

    def near_here(n, sign):
        dc, dg = sign * NEAR[n][0], sign * NEAR[n][1]
        ok = (c + dc >= 0) & (c + dc < parts)
        return ok & (g + dg >= 0) & (g + dg < groups)

    def first_copy(j, step):
        to = (g + step) % groups
        return pltpu.make_async_remote_copy(
            src_ref=ext.at[j, pl.ds(1, 2), 1, pl.ds(1, group)],
            dst_ref=first.at[j, :, pl.ds(g * group, group)],
            send_sem=f_send.at[j, step - 1],
            recv_sem=f_recv.at[j, g],
            device_id=(c, to * group + m),
            device_id_type=MESH,
        )

    def first_got(j, step):
        come = (g + step) % groups
        return pltpu.make_async_remote_copy(
            src_ref=ext.at[j, pl.ds(1, 2), 1, pl.ds(1, group)],
            dst_ref=first.at[j, :, pl.ds(come * group, group)],
            send_sem=f_send.at[j, step - 1],
            recv_sem=f_recv.at[j, come],
            device_id=(c, come * group + m),
            device_id_type=MESH,
        )

    def first_on(j, to):
        return pltpu.make_async_remote_copy(
            src_ref=first.at[j],
            dst_ref=first.at[j],
            send_sem=t_send.at[j, to - 1],
            recv_sem=t_recv.at[j],
            device_id=(to, at),
            device_id_type=MESH,
        )

    def columns(head):
        return pl.ds(pl.multiple_of(head * dim, dim), dim)

    def out_copy(j, step):
        to = peer(step)
        return pltpu.make_async_remote_copy(
            src_ref=held.at[j, to],
            dst_ref=out_ref.at[:, columns(m * heads + j)],
            send_sem=o_send.at[j, step - 1],
            recv_sem=o_recv.at[j, m],
            device_id=(c, g * group + to),
            device_id_type=MESH,
        )

    def out_got(j, step):
        come = peer(step)
        return pltpu.make_async_remote_copy(
            src_ref=held.at[j, come],
            dst_ref=out_ref.at[:, columns(come * heads + j)],
            send_sem=o_send.at[j, step - 1],
            recv_sem=o_recv.at[j, come],
            device_id=(c, g * group + come),
            device_id_type=MESH,
        )

    def mask_copy(step):
        return pltpu.make_async_remote_copy(
            src_ref=mask_ref,
            dst_ref=masks.at[m],
            send_sem=m_send.at[step - 1],
            recv_sem=m_recv.at[m],
            device_id=(c, g * group + peer(step)),
            device_id_type=MESH,
        )

    def mask_got(step):
        come = peer(step)
        return pltpu.make_async_remote_copy(
            src_ref=mask_ref,
            dst_ref=masks.at[come],
            send_sem=m_send.at[step - 1],
            recv_sem=m_recv.at[come],
            device_id=(c, g * group + come),
            device_id_type=MESH,
        )

    def turned(ref, head):
        x = ref[:, columns(head)].astype(jnp.float32)
        y = x * cos_ref[...] + pltpu.roll(x, dim // 2, 1) * sin_ref[...]
        return y.astype(jnp.bfloat16).reshape(frames, width, dim)

    def share(j):
        for step in range(1, group):
            head = peer(step) * heads + j
            rot[head, 0] = turned(q_ref, head)
            rot[head, 1] = turned(k_ref, head)
            rot[head, 2] = v_ref[:, columns(head)].reshape(frames, width, dim)
            send_rows(j, step).start()
        head = m * heads + j
        ext[j, 0, pl.ds(1, frames), m + 1] = turned(q_ref, head)
        ext[j, 1, pl.ds(1, frames), m + 1] = turned(k_ref, head)
        ext[j, 2, pl.ds(1, frames), m + 1] = v_ref[:, columns(head)].reshape(frames, width, dim)

    def clear(part):
        part[...] = jnp.zeros(part.shape, part.dtype)

    pl.when(c == 0)(lambda: clear(ext.at[:, pl.ds(1, 2), 0]))
    pl.when(c == parts - 1)(lambda: clear(ext.at[:, pl.ds(1, 2), frames + 1]))
    pl.when(g == 0)(lambda: clear(ext.at[:, pl.ds(1, 2), :, 0]))
    pl.when(g == groups - 1)(lambda: clear(ext.at[:, pl.ds(1, 2), :, group + 1]))

    barrier = pltpu.get_barrier_semaphore()
    for step in range(1, group):
        pl.semaphore_signal(barrier, inc=1, device_id=(c, g * group + peer(step)), device_id_type=MESH)
    for dt in range(parts):
        for dg in range(groups):
            if (dt, dg) != (0, 0):
                to = ((c + dt) % parts, (g + dg) % groups * group + m)
                pl.semaphore_signal(barrier, inc=1, device_id=to, device_id_type=MESH)
    pl.semaphore_wait(barrier, group - 1 + parts * groups - 1)

    for step in range(1, group):
        mask_copy(step).start()
    masks[m] = mask_ref[...]
    lax.fori_loop(0, min(2, heads), lambda j, x: (share(j), x)[1], 0)

    def spread_on(s):
        for step in range(1, group):
            got_rows(s, step).wait_recv()

        @pl.when(c == 0)
        def _():
            for step in range(1, groups):
                first_copy(s, step).start()

        for n in range(len(NEAR)):
            pl.when(near_here(n, 1))(lambda n=n: near_copy(s, n).start())

        pl.when(s + 2 < heads)(lambda: share(s + 2))

        @pl.when(c == 0)
        def _():
            first[s, :, pl.ds(g * group, group)] = ext[s, pl.ds(1, 2), 1, pl.ds(1, group)]

    def make_bias():
        for step in range(1, group):
            mask_got(step).wait_recv()
        for row in range(group):
            spread = jnp.concatenate(
                [jnp.broadcast_to(masks[row, f : f + 1, :], (width, masks.shape[2])) * own_ref[...] for f in range(frames)],
                axis=0,
            ).astype(jnp.bfloat16)
            allowed = jnp.dot(spread, pick_ref[row], preferred_element_type=jnp.float32)
            allowed = (allowed - 1.0) * 1e30
            bias[:, pl.ds(row * width, width)] = allowed.reshape(frames, width, allowed.shape[1])

    factor = math.log2(math.e) / math.sqrt(dim)

    def attend(j):
        @pl.when(c == 0)
        def _():
            for step in range(1, groups):
                first_got(j, step).wait_recv()
            for to in range(1, parts):
                first_on(j, to).start()

        pl.when(c > 0)(lambda: first_on(j, 1).wait_recv())
        for n in range(len(NEAR)):
            pl.when(near_here(n, -1))(lambda n=n: near_copy(j, n).wait_recv())

        far_k = first[j, 0].reshape(-1, dim)
        far_v = first[j, 1].reshape(-1, dim)
        far_v = jnp.concatenate([far_v, jnp.ones_like(far_v)], axis=1)
        last = (((1,), (1,)), ((), ()))
        for f in range(frames):
            q = ext[j, 0, 1 + f, pl.ds(1, group)].reshape(tokens, dim)
            near_k = ext[j, 1, pl.ds(f, 3)].reshape(-1, dim)
            near_v = ext[j, 2, pl.ds(f, 3)].reshape(-1, dim)
            near_v = jnp.concatenate([near_v, jnp.ones_like(near_v)], axis=1)
            s_near = lax.dot_general(q, near_k, last, preferred_element_type=jnp.float32) + bias[f]
            s_far = lax.dot_general(q, far_k, last, preferred_element_type=jnp.float32)
            top = jnp.maximum(
                jnp.max(s_near, axis=1, keepdims=True), jnp.max(s_far, axis=1, keepdims=True)
            )
            p_near = jnp.exp2((s_near - top) * factor).astype(jnp.bfloat16)
            p_far = jnp.exp2((s_far - top) * factor).astype(jnp.bfloat16)
            both = jnp.dot(p_near, near_v, preferred_element_type=jnp.float32)
            both = both + jnp.dot(p_far, far_v, preferred_element_type=jnp.float32)
            result = (both[:, :dim] / both[:, dim:]).astype(jnp.bfloat16)
            held[j, :, pl.ds(f * width, width)] = result.reshape(group, width, dim)
        for step in range(1, group):
            out_copy(j, step).start()
        out_ref[:, columns(m * heads + j)] = held[j, m]

    def turn(s, carry):
        pl.when(s < heads)(lambda: spread_on(s))
        pl.when(s == 0)(make_bias)
        pl.when(s > 0)(lambda: attend(s - 1))
        return carry

    lax.fori_loop(0, heads + 1, turn, 0)

    def finish(j, carry):
        for step in range(1, group):
            send_rows(j, step).wait_send()
            out_copy(j, step).wait_send()
            out_got(j, step).wait_recv()
        for n in range(len(NEAR)):
            pl.when(near_here(n, 1))(lambda n=n: near_copy(j, n).wait_send())

        @pl.when(c == 0)
        def _():
            for step in range(1, groups):
                first_copy(j, step).wait_send()
            for to in range(1, parts):
                first_on(j, to).wait_send()

        return carry

    lax.fori_loop(0, heads, finish, 0)
    for step in range(1, group):
        mask_copy(step).wait_send()


def per_device(parts, high, queries, keys, values, window_mask, pos_t, pos_h, pos_w):
    frames, row_count, width, channels = queries.shape
    assert row_count == 1
    dim = HEAD_DIM
    group = next(n for n in (4, 2, 1) if HEADS % n == 0 and high % n == 0)
    groups, heads = high // group, HEADS // group
    blocks = width // TILE_W
    lanes = 128
    cos_tab, sine_tab = rope_tables(pos_t, pos_h, pos_w, dim // 2)
    tokens = frames * width
    mask = jnp.pad((window_mask[:, 0] > 0).astype(jnp.float32), ((0, 0), (0, 0), (0, lanes // blocks - 27)))
    mask_rows = -(-frames // 8) * 8
    mask = jnp.pad(mask.reshape(frames, lanes), ((0, mask_rows - frames), (0, 0)))
    own, pick = mask_selectors(group, width, lanes)
    keys_near = pick.shape[2]
    sem = pltpu.SemaphoreType.DMA
    out = pl.pallas_call(
        functools.partial(kernel, (group, groups, parts, frames, width, heads)),
        out_shape=jax.ShapeDtypeStruct((tokens, channels), jnp.bfloat16),
        in_specs=[pl.BlockSpec(memory_space=pltpu.VMEM)] * 8,
        out_specs=pl.BlockSpec(memory_space=pltpu.VMEM),
        scratch_shapes=[
            pltpu.VMEM((HEADS, 3, frames, width, dim), jnp.bfloat16),
            pltpu.VMEM((heads, 3, frames + 2, group + 2, width, dim), jnp.bfloat16),
            pltpu.VMEM((heads, 2, high, width, dim), jnp.bfloat16),
            pltpu.VMEM((heads, group, tokens, dim), jnp.bfloat16),
            pltpu.VMEM((group, mask_rows, lanes), jnp.float32),
            pltpu.VMEM((frames, group * width, keys_near), jnp.float32),
            sem((heads, max(1, group - 1))),
            sem((heads, group)),
            sem((heads, len(NEAR))),
            sem((heads, len(NEAR))),
            sem((heads, max(1, groups - 1))),
            sem((heads, groups)),
            sem((heads, max(1, parts - 1))),
            sem((heads,)),
            sem((heads, max(1, group - 1))),
            sem((heads, group)),
            sem((max(1, group - 1),)),
            sem((group,)),
        ],
        compiler_params=pltpu.CompilerParams(
            collective_id=0, has_side_effects=True, vmem_limit_bytes=48 * 1024 * 1024
        ),
    )(
        queries.reshape(tokens, channels),
        keys.reshape(tokens, channels),
        values.reshape(tokens, channels),
        cos_tab.reshape(tokens, dim),
        sine_tab.reshape(tokens, dim),
        mask,
        jnp.asarray(own),
        jnp.asarray(pick, jnp.bfloat16),
    )
    return out.reshape(queries.shape)


def solution(mesh):
    return jax.shard_map(
        functools.partial(per_device, mesh.shape["tm"], mesh.shape["height"]),
        mesh=mesh,
        in_specs=(
            P("tm", "height", None, None),
            P("tm", "height", None, None),
            P("tm", "height", None, None),
            P("tm", "height", None, None),
            P("tm"),
            P("height"),
            P(),
        ),
        out_specs=P("tm", "height", None, None),
        check_vma=False,
    )
```

profile of v0, /device:TPU:0, one launch (start us, length us, event | category | flops | bytes accessed | tf_op | source)
XLA Modules:
  0.0 50.8 jit_solution(17468120248500786852)
XLA Ops:
  0.0 0.0 copy-start.5
  0.0 0.0 copy-start
  0.7 0.7 %convert_element_type.34 = f32[4]{0:T(128)S(1)} convert(s32[4]{0:T(128)} %param.13) | non-fusion elementwise | flops 4 | bytes 32 | tf_op jit(solution)/shard_map/convert_element_type | solution.py:34
  1.4 0.7 %convert_element_type.37 = f32[32]{0:T(128)S(1)} convert(s32[32]{0:T(128)} %param.15) | non-fusion elementwise | flops 32 | bytes 256 | tf_op jit(solution)/shard_map/convert_element_type | solution.py:36
  2.1 0.1 multiply_add_fusion
  2.1 0.0 copy-done.5
  2.2 0.1 reshape.156
  2.3 0.1 broadcast_multiply_fusion
  2.3 0.2 add_sine_fusion
  2.6 0.1 pad_maximum_fusion.cos_ref
  2.7 0.0 copy-start.4
  2.7 0.1 pad_maximum_fusion.1.sin_ref
  2.8 0.0 copy-done
  2.8 0.6 %copy-done.4 = f32[32,128]{1,0:T(8,128)S(1)} copy-done((f32[32,128]{1,0:T(8,128)S(1)}, f32[32,128]{1,0:T(8,128)}, u32[]{:S(2)}) %copy-start.4) | copy-done | bytes 16408
  3.4 0.0 copy-start.1
  3.4 1.1 %copy-done.1 = bf16[4,1,32,2560]{3,2,1,0:T(8,128)(2,1)S(1)} copy-done((bf16[4,1,32,2560]{3,2,1,0:T(8,128)(2,1)S(1)}, bf16[4,1,32,2560]{3,2,1,0:T(8,128)(2,1)}, u32[]{:S(2)}) %copy-start.1) | copy-done | bytes 655384
  4.5 0.0 copy-start.2
  4.5 1.1 %copy-done.2 = bf16[4,1,32,2560]{3,2,1,0:T(8,128)(2,1)S(1)} copy-done((bf16[4,1,32,2560]{3,2,1,0:T(8,128)(2,1)S(1)}, bf16[4,1,32,2560]{3,2,1,0:T(8,128)(2,1)}, u32[]{:S(2)}) %copy-start.2) | copy-done | bytes 655384
  5.6 0.0 copy-start.3
  5.6 1.1 %copy-done.3 = bf16[4,128,576]{2,1,0:T(8,128)(2,1)S(1)} copy-done((bf16[4,128,576]{2,1,0:T(8,128)(2,1)S(1)}, bf16[4,128,576]{2,1,0:T(8,128)(2,1)}, u32[]{:S(2)}) %copy-start.3) | copy-done | bytes 589848
  6.7 43.3 %shard_map.91 = bf16[128,2560]{1,0:T(8,128)(2,1)S(1)} custom-call(bf16[128,2560]{1,0:T(8,128)(2,1)S(1)} %bitcast.13, bf16[128,2560]{1,0:T(8,128)(2,1)S(1)} %bitcast.14, bf16[128,2560]{1,0:T(8,128)(2,1)S(1)} %bitcast.15, f32[128,128]{1,0:T(8,128)S(1)} %pad_maximum_fusion.cos_ref, f32[128,128]{1,0:T(8,128)S(1)} %pad_maximum_fusion.1.sin_ref, ...), custom_call_target="tpu_custom_call" | custom-call | tf_op jit(solution)/shard_map/pallas_call | solution.py:353
  50.0 0.8 %copy.13 = bf16[4,1,32,2560]{3,2,1,0:T(8,128)(2,1)} copy(bf16[4,1,32,2560]{3,2,1,0:T(8,128)(2,1)S(1)} %bitcast.12) | data formatting | bytes 1310720
  (6 shorter events, 0.0 us)
Async XLA Ops:
  0.0 2.1 %copy-start.5 = (s32[4,1,4,27]{3,2,1,0:T(4,128)S(1)}, s32[4,1,4,27]{3,2,1,0:T(4,128)}, u32[]{:S(2)}) copy-start(s32[4,1,4,27]{3,2,1,0:T(4,128)} %param.12) | copy-start | bytes 5188
  0.0 2.8 %copy-start = (bf16[4,1,32,2560]{3,2,1,0:T(8,128)(2,1)S(1)}, bf16[4,1,32,2560]{3,2,1,0:T(8,128)(2,1)}, u32[]{:S(2)}) copy-start(bf16[4,1,32,2560]{3,2,1,0:T(8,128)(2,1)} %param.9) | copy-start | bytes 1966084
  2.7 0.7 %copy-start.4 = (f32[32,128]{1,0:T(8,128)S(1)}, f32[32,128]{1,0:T(8,128)}, u32[]{:S(2)}) copy-start(f32[32,128]{1,0:T(8,128)} %constant.29.clone.own_ref) | copy-start | bytes 49156
  3.4 1.1 %copy-start.1 = (bf16[4,1,32,2560]{3,2,1,0:T(8,128)(2,1)S(1)}, bf16[4,1,32,2560]{3,2,1,0:T(8,128)(2,1)}, u32[]{:S(2)}) copy-start(bf16[4,1,32,2560]{3,2,1,0:T(8,128)(2,1)} %param.10) | copy-start | bytes 1966084
  4.5 1.1 %copy-start.2 = (bf16[4,1,32,2560]{3,2,1,0:T(8,128)(2,1)S(1)}, bf16[4,1,32,2560]{3,2,1,0:T(8,128)(2,1)}, u32[]{:S(2)}) copy-start(bf16[4,1,32,2560]{3,2,1,0:T(8,128)(2,1)} %param.11) | copy-start | bytes 1966084
  5.6 1.1 %copy-start.3 = (bf16[4,128,576]{2,1,0:T(8,128)(2,1)S(1)}, bf16[4,128,576]{2,1,0:T(8,128)(2,1)}, u32[]{:S(2)}) copy-start(bf16[4,128,576]{2,1,0:T(8,128)(2,1)} %constant.30.clone.pick_ref) | copy-start | bytes 1769476
where the time goes:
time: 51.1 us; the launch traced here: 50.8 us
  Pallas kernels  43.3 us (85%)
  local copies, waits for them, and re-layouts  4.81 us (9%)
  other arithmetic  1.9 us (4%)
  between operations  0.8 us (2%)
    pallas_call x1, Pallas kernels, per_device(): pl.pallas_call(functools.partial(kernel, (group, groups, parts, frames, w...  43.3 us
    unnamed x13, local copies, waits for them, and re-layouts  4.72 us

commit v1 on v0

--- a/solution.py
+++ b/solution.py
@@ -16,28 +16,16 @@
 NEAR = [(dc, dg) for dc in (-1, 0, 1) for dg in (-1, 0, 1) if (dc, dg) != (0, 0)]
 
 
-def rope_tables(pos_t, pos_h, pos_w, half_dim):
+def frequencies(half_dim):
     pairs_hw = 2 * half_dim // 6
     pairs_time = half_dim - 2 * pairs_hw
-    pair_index = jnp.arange(half_dim).astype(jnp.float32)
-    freq_time = jnp.where(
-        pair_index < pairs_time, jnp.power(10000.0, -pair_index / pairs_time), 0.0
-    )
-    in_rows = (pair_index >= pairs_time) & (pair_index < pairs_time + pairs_hw)
-    freq_rows = jnp.where(in_rows, jnp.power(10000.0, -(pair_index - pairs_time) / pairs_hw), 0.0)
-    freq_cols = jnp.where(
-        pair_index >= pairs_time + pairs_hw,
-        jnp.power(10000.0, -(pair_index - pairs_time - pairs_hw) / pairs_hw),
-        0.0,
-    )
-    angles = (
-        pos_t.astype(jnp.float32)[:, None, None, None] * freq_time
-        + pos_h.astype(jnp.float32)[None, :, None, None] * freq_rows
-        + pos_w.astype(jnp.float32)[None, None, :, None] * freq_cols
-    )
-    cos_tab = jnp.cos(angles)
-    sine_tab = jnp.sin(angles)
-    return (jnp.concatenate([cos_tab, cos_tab], -1), jnp.concatenate([-sine_tab, sine_tab], -1))
+    pair = np.arange(2 * half_dim) % half_dim
+    count = np.where(pair < pairs_time, pairs_time, pairs_hw)
+    first = np.where(pair < pairs_time, 0, np.where(pair < pairs_time + pairs_hw, pairs_time, pairs_time + pairs_hw))
+    freq = 10000.0 ** (-(pair - first) / count)
+    sign = np.where(np.arange(2 * half_dim) < half_dim, -1.0, 1.0)
+    rows = [np.where(first == start, freq, 0.0) for start in (0, pairs_time, pairs_time + pairs_hw)]
+    return np.stack(rows + [sign]).astype(np.float32)
 
 
 def mask_selectors(group, width, lanes):
@@ -61,9 +49,10 @@
 
 
 def kernel(
-    sizes, q_ref, k_ref, v_ref, cos_ref, sin_ref, mask_ref, own_ref, pick_ref, out_ref,
-    rot, ext, first, held, masks, bias,
-    a_send, a_recv, n_send, n_recv, f_send, f_recv, t_send, t_recv, o_send, o_recv, m_send, m_recv,
+    sizes, q_hbm, k_hbm, v_hbm, mask_hbm, pos_t_hbm, pos_h_ref, pos_w_hbm, const_hbm, pick_hbm, out_ref,
+    q_ref, k_ref, v_ref, mask_in, pos_t_ref, pos_w_ref, const_ref, pick_ref,
+    cos_ref, sin_ref, mask_pad, mask_ref, q_rot, rot, q_all, ext, first, held, masks, bias,
+    load, q_send, q_recv, a_send, a_recv, n_send, n_recv, f_send, f_recv, t_send, t_recv, o_send, o_recv, m_send, m_recv,
 ):
     group, groups, parts, frames, width, heads = sizes
     dim = HEAD_DIM
@@ -76,25 +65,27 @@
     def peer(step):
         return (m + step) % group
 
-    def send_rows(j, step):
-        to = peer(step)
-        return pltpu.make_async_remote_copy(
-            src_ref=rot.at[to * heads + j],
-            dst_ref=ext.at[j, :, pl.ds(1, frames), m + 1],
+    def row_copy(j, step, landing):
+        other = peer(step)
+        row = other if landing else m
+        return pltpu.make_async_remote_copy(
+            src_ref=rot.at[other * heads + j],
+            dst_ref=ext.at[j, :, pl.ds(1, frames), row + 1],
             send_sem=a_send.at[j, step - 1],
-            recv_sem=a_recv.at[j, m],
-            device_id=(c, g * group + to),
-            device_id_type=MESH,
-        )
-
-    def got_rows(j, step):
-        come = peer(step)
-        return pltpu.make_async_remote_copy(
-            src_ref=rot.at[come * heads + j],
-            dst_ref=ext.at[j, :, pl.ds(1, frames), come + 1],
-            send_sem=a_send.at[j, step - 1],
-            recv_sem=a_recv.at[j, come],
-            device_id=(c, g * group + come),
+            recv_sem=a_recv.at[j, row],
+            device_id=(c, g * group + other),
+            device_id_type=MESH,
+        )
+
+    def query_copy(j, step, landing):
+        other = peer(step)
+        row = other if landing else m
+        return pltpu.make_async_remote_copy(
+            src_ref=q_rot.at[other * heads + j],
+            dst_ref=q_all.at[j, :, row],
+            send_sem=q_send.at[j, step - 1],
+            recv_sem=q_recv.at[j, row],
+            device_id=(c, g * group + other),
             device_id_type=MESH,
         )
 
@@ -105,8 +96,8 @@
         src_h = {-1: pl.ds(1, 1), 0: pl.ds(1, group), 1: pl.ds(group, 1)}[dg]
         dst_h = {-1: pl.ds(group + 1, 1), 0: pl.ds(1, group), 1: pl.ds(0, 1)}[dg]
         return pltpu.make_async_remote_copy(
-            src_ref=ext.at[j, pl.ds(1, 2), src_t, src_h],
-            dst_ref=ext.at[j, pl.ds(1, 2), dst_t, dst_h],
+            src_ref=ext.at[j, :, src_t, src_h],
+            dst_ref=ext.at[j, :, dst_t, dst_h],
             send_sem=n_send.at[j, n],
             recv_sem=n_recv.at[j, n],
             device_id=(c + dc, at + dg * group),
@@ -121,7 +112,7 @@
     def first_copy(j, step):
         to = (g + step) % groups
         return pltpu.make_async_remote_copy(
-            src_ref=ext.at[j, pl.ds(1, 2), 1, pl.ds(1, group)],
+            src_ref=ext.at[j, :, 1, pl.ds(1, group)],
             dst_ref=first.at[j, :, pl.ds(g * group, group)],
             send_sem=f_send.at[j, step - 1],
             recv_sem=f_recv.at[j, g],
@@ -132,7 +123,7 @@
     def first_got(j, step):
         come = (g + step) % groups
         return pltpu.make_async_remote_copy(
-            src_ref=ext.at[j, pl.ds(1, 2), 1, pl.ds(1, group)],
+            src_ref=ext.at[j, :, 1, pl.ds(1, group)],
             dst_ref=first.at[j, :, pl.ds(come * group, group)],
             send_sem=f_send.at[j, step - 1],
             recv_sem=f_recv.at[j, come],
@@ -197,29 +188,35 @@
         )
 
     def turned(ref, head):
-        x = ref[:, columns(head)].astype(jnp.float32)
+        x = ref[:, 0, :, columns(head)].astype(jnp.float32).reshape(frames * width, dim)
         y = x * cos_ref[...] + pltpu.roll(x, dim // 2, 1) * sin_ref[...]
         return y.astype(jnp.bfloat16).reshape(frames, width, dim)
 
-    def share(j):
+    def make_rows(j):
         for step in range(1, group):
             head = peer(step) * heads + j
-            rot[head, 0] = turned(q_ref, head)
-            rot[head, 1] = turned(k_ref, head)
-            rot[head, 2] = v_ref[:, columns(head)].reshape(frames, width, dim)
-            send_rows(j, step).start()
+            rot[head, 0] = turned(k_ref, head)
+            rot[head, 1] = v_ref[:, 0, :, columns(head)]
         head = m * heads + j
-        ext[j, 0, pl.ds(1, frames), m + 1] = turned(q_ref, head)
-        ext[j, 1, pl.ds(1, frames), m + 1] = turned(k_ref, head)
-        ext[j, 2, pl.ds(1, frames), m + 1] = v_ref[:, columns(head)].reshape(frames, width, dim)
+        ext[j, 0, pl.ds(1, frames), m + 1] = turned(k_ref, head)
+        ext[j, 1, pl.ds(1, frames), m + 1] = v_ref[:, 0, :, columns(head)]
+
+    def send_rows(j):
+        for step in range(1, group):
+            row_copy(j, step, False).start()
+
+    def make_queries(j):
+        for step in range(1, group):
+            head = peer(step) * heads + j
+            q_rot[head] = turned(q_ref, head)
+        q_all[j, :, m] = turned(q_ref, m * heads + j)
+
+    def send_queries(j):
+        for step in range(1, group):
+            query_copy(j, step, False).start()
 
     def clear(part):
         part[...] = jnp.zeros(part.shape, part.dtype)
-
-    pl.when(c == 0)(lambda: clear(ext.at[:, pl.ds(1, 2), 0]))
-    pl.when(c == parts - 1)(lambda: clear(ext.at[:, pl.ds(1, 2), frames + 1]))
-    pl.when(g == 0)(lambda: clear(ext.at[:, pl.ds(1, 2), :, 0]))
-    pl.when(g == groups - 1)(lambda: clear(ext.at[:, pl.ds(1, 2), :, group + 1]))
 
     barrier = pltpu.get_barrier_semaphore()
     for step in range(1, group):
@@ -229,16 +226,78 @@
             if (dt, dg) != (0, 0):
                 to = ((c + dt) % parts, (g + dg) % groups * group + m)
                 pl.semaphore_signal(barrier, inc=1, device_id=to, device_id_type=MESH)
+
+    loads = [
+        pltpu.make_async_copy(src, dst, load.at[n])
+        for n, (src, dst) in enumerate(
+            [
+                (const_hbm, const_ref), (pos_t_hbm, pos_t_ref), (pos_w_hbm, pos_w_ref),
+                (mask_hbm, mask_in), (k_hbm, k_ref), (v_hbm, v_ref), (q_hbm, q_ref), (pick_hbm, pick_ref),
+            ]
+        )
+    ]
+    for copy in loads:
+        copy.start()
+
+    pl.when(c == 0)(lambda: clear(ext.at[:, :, 0]))
+    pl.when(c == parts - 1)(lambda: clear(ext.at[:, :, frames + 1]))
+    pl.when(g == 0)(lambda: clear(ext.at[:, :, :, 0]))
+    pl.when(g == groups - 1)(lambda: clear(ext.at[:, :, :, group + 1]))
+    clear(mask_pad)
+
+    for copy in loads[:4]:
+        copy.wait()
+
+    def column(ref, rows):
+        row = ref[...].astype(jnp.float32)
+        spread = jnp.broadcast_to(row, (rows, row.shape[1]))
+        here = lax.broadcasted_iota(jnp.int32, spread.shape, 0) == lax.broadcasted_iota(jnp.int32, spread.shape, 1)
+        return jnp.sum(jnp.where(here, spread, 0.0), axis=1, keepdims=True)
+
+    freq_t = const_ref[width : width + 1, :]
+    freq_h = const_ref[width + 1 : width + 2, :]
+    freq_w = const_ref[width + 2 : width + 3, :]
+    sign = const_ref[width + 3 : width + 4, :]
+    pos_h = pos_h_ref[0].astype(jnp.float32)
+    angle_hw = pos_h * freq_h + column(pos_w_ref, width) * freq_w
+    angle_t = column(pos_t_ref, mask_ref.shape[0]) * freq_t
+    for table, of, factor in ((cos_ref, jnp.cos, None), (sin_ref, jnp.sin, sign)):
+        of_hw, of_t = of(angle_hw), of(angle_t)
+        for f in range(frames):
+            part = jnp.where(freq_t > 0, of_t[f : f + 1, :], of_hw)
+            table[pl.ds(f * width, width), :] = part if factor is None else part * factor
+    slot = mask_ref.shape[1] // mask_in.shape[2]
+    for f in range(frames):
+        mask_pad[f, pl.ds(0, mask_in.shape[2]), pl.ds(0, mask_in.shape[3])] = (mask_in[f, 0] > 0).astype(jnp.float32)
+    clear(mask_ref)
+    for f in range(frames):
+        tile_rows = mask_pad[f]
+        line = tile_rows[0:1, :]
+        for b in range(1, mask_in.shape[2]):
+            line = line + pltpu.roll(tile_rows, b * slot, 1)[b : b + 1, :]
+        mask_ref[f : f + 1, :] = line
+    masks[m] = mask_ref[...]
+
+    loads[4].wait()
+    loads[5].wait()
+    make_rows(0)
     pl.semaphore_wait(barrier, group - 1 + parts * groups - 1)
-
+    send_rows(0)
+    if heads > 1:
+        make_rows(1)
+        send_rows(1)
+    loads[6].wait()
+    make_queries(0)
+    send_queries(0)
+    if heads > 2:
+        make_rows(2)
+        send_rows(2)
     for step in range(1, group):
         mask_copy(step).start()
-    masks[m] = mask_ref[...]
-    lax.fori_loop(0, min(2, heads), lambda j, x: (share(j), x)[1], 0)
 
     def spread_on(s):
         for step in range(1, group):
-            got_rows(s, step).wait_recv()
+            row_copy(s, step, True).wait_recv()
 
         @pl.when(c == 0)
         def _():
@@ -248,18 +307,28 @@
         for n in range(len(NEAR)):
             pl.when(near_here(n, 1))(lambda n=n: near_copy(s, n).start())
 
-        pl.when(s + 2 < heads)(lambda: share(s + 2))
+        def more_rows():
+            make_rows(s + 3)
+            send_rows(s + 3)
+
+        def more_queries():
+            make_queries(s + 1)
+            send_queries(s + 1)
+
+        pl.when(s + 3 < heads)(more_rows)
+        pl.when(s + 1 < heads)(more_queries)
 
         @pl.when(c == 0)
         def _():
-            first[s, :, pl.ds(g * group, group)] = ext[s, pl.ds(1, 2), 1, pl.ds(1, group)]
+            first[s, :, pl.ds(g * group, group)] = ext[s, :, 1, pl.ds(1, group)]
 
     def make_bias():
         for step in range(1, group):
             mask_got(step).wait_recv()
+        loads[7].wait()
         for row in range(group):
             spread = jnp.concatenate(
-                [jnp.broadcast_to(masks[row, f : f + 1, :], (width, masks.shape[2])) * own_ref[...] for f in range(frames)],
+                [jnp.broadcast_to(masks[row, f : f + 1, :], (width, masks.shape[2])) * const_ref[0:width, :] for f in range(frames)],
                 axis=0,
             ).astype(jnp.bfloat16)
             allowed = jnp.dot(spread, pick_ref[row], preferred_element_type=jnp.float32)
@@ -280,14 +349,16 @@
         for n in range(len(NEAR)):
             pl.when(near_here(n, -1))(lambda n=n: near_copy(j, n).wait_recv())
 
+        for step in range(1, group):
+            query_copy(j, step, True).wait_recv()
         far_k = first[j, 0].reshape(-1, dim)
         far_v = first[j, 1].reshape(-1, dim)
         far_v = jnp.concatenate([far_v, jnp.ones_like(far_v)], axis=1)
         last = (((1,), (1,)), ((), ()))
         for f in range(frames):
-            q = ext[j, 0, 1 + f, pl.ds(1, group)].reshape(tokens, dim)
-            near_k = ext[j, 1, pl.ds(f, 3)].reshape(-1, dim)
-            near_v = ext[j, 2, pl.ds(f, 3)].reshape(-1, dim)
+            q = q_all[j, f].reshape(tokens, dim)
+            near_k = ext[j, 0, pl.ds(f, 3)].reshape(-1, dim)
+            near_v = ext[j, 1, pl.ds(f, 3)].reshape(-1, dim)
             near_v = jnp.concatenate([near_v, jnp.ones_like(near_v)], axis=1)
             s_near = lax.dot_general(q, near_k, last, preferred_element_type=jnp.float32) + bias[f]
             s_far = lax.dot_general(q, far_k, last, preferred_element_type=jnp.float32)
@@ -314,7 +385,8 @@
 
     def finish(j, carry):
         for step in range(1, group):
-            send_rows(j, step).wait_send()
+            row_copy(j, step, False).wait_send()
+            query_copy(j, step, False).wait_send()
             out_copy(j, step).wait_send()
             out_got(j, step).wait_recv()
         for n in range(len(NEAR)):
@@ -342,26 +414,42 @@
     groups, heads = high // group, HEADS // group
     blocks = width // TILE_W
     lanes = 128
-    cos_tab, sine_tab = rope_tables(pos_t, pos_h, pos_w, dim // 2)
     tokens = frames * width
-    mask = jnp.pad((window_mask[:, 0] > 0).astype(jnp.float32), ((0, 0), (0, 0), (0, lanes // blocks - 27)))
     mask_rows = -(-frames // 8) * 8
-    mask = jnp.pad(mask.reshape(frames, lanes), ((0, mask_rows - frames), (0, 0)))
     own, pick = mask_selectors(group, width, lanes)
+    const = np.concatenate([own, frequencies(dim // 2)], axis=0)
+    const = np.pad(const, ((0, -len(const) % 8), (0, 0)))
     keys_near = pick.shape[2]
     sem = pltpu.SemaphoreType.DMA
     out = pl.pallas_call(
         functools.partial(kernel, (group, groups, parts, frames, width, heads)),
         out_shape=jax.ShapeDtypeStruct((tokens, channels), jnp.bfloat16),
-        in_specs=[pl.BlockSpec(memory_space=pltpu.VMEM)] * 8,
+        in_specs=[pl.BlockSpec(memory_space=pltpu.SMEM if n == 5 else pltpu.HBM) for n in range(9)],
         out_specs=pl.BlockSpec(memory_space=pltpu.VMEM),
         scratch_shapes=[
-            pltpu.VMEM((HEADS, 3, frames, width, dim), jnp.bfloat16),
-            pltpu.VMEM((heads, 3, frames + 2, group + 2, width, dim), jnp.bfloat16),
+            pltpu.VMEM(queries.shape, jnp.bfloat16),
+            pltpu.VMEM(queries.shape, jnp.bfloat16),
+            pltpu.VMEM(queries.shape, jnp.bfloat16),
+            pltpu.VMEM(window_mask.shape, jnp.int32),
+            pltpu.VMEM((1, frames), jnp.int32),
+            pltpu.VMEM((1, width), jnp.int32),
+            pltpu.VMEM(const.shape, jnp.float32),
+            pltpu.VMEM(pick.shape, jnp.bfloat16),
+            pltpu.VMEM((tokens, dim), jnp.float32),
+            pltpu.VMEM((tokens, dim), jnp.float32),
+            pltpu.VMEM((frames, -(-blocks // 8) * 8, lanes), jnp.float32),
+            pltpu.VMEM((mask_rows, lanes), jnp.float32),
+            pltpu.VMEM((HEADS, frames, width, dim), jnp.bfloat16),
+            pltpu.VMEM((HEADS, 2, frames, width, dim), jnp.bfloat16),
+            pltpu.VMEM((heads, frames, group, width, dim), jnp.bfloat16),
+            pltpu.VMEM((heads, 2, frames + 2, group + 2, width, dim), jnp.bfloat16),
             pltpu.VMEM((heads, 2, high, width, dim), jnp.bfloat16),
             pltpu.VMEM((heads, group, tokens, dim), jnp.bfloat16),
             pltpu.VMEM((group, mask_rows, lanes), jnp.float32),
             pltpu.VMEM((frames, group * width, keys_near), jnp.float32),
+            sem((8,)),
+            sem((heads, max(1, group - 1))),
+            sem((heads, group)),
             sem((heads, max(1, group - 1))),
             sem((heads, group)),
             sem((heads, len(NEAR))),
@@ -376,16 +464,17 @@
             sem((group,)),
         ],
         compiler_params=pltpu.CompilerParams(
-            collective_id=0, has_side_effects=True, vmem_limit_bytes=48 * 1024 * 1024
+            collective_id=0, has_side_effects=True, vmem_limit_bytes=62 * 1024 * 1024
         ),
     )(
-        queries.reshape(tokens, channels),
-        keys.reshape(tokens, channels),
-        values.reshape(tokens, channels),
-        cos_tab.reshape(tokens, dim),
-        sine_tab.reshape(tokens, dim),
-        mask,
-        jnp.asarray(own),
+        queries,
+        keys,
+        values,
+        window_mask,
+        pos_t.reshape(1, -1),
+        pos_h,
+        pos_w.reshape(1, -1),
+        jnp.asarray(const),
         jnp.asarray(pick, jnp.bfloat16),
     )
     return out.reshape(queries.shape)

time: 51.1 us -> 49 us (0.959)
  Pallas kernels: 43.3 us -> 46.2 us
  local copies, waits for them, and re-layouts: 4.81 us -> 1.97 us
  other arithmetic: 1.9 us -> 0 us
    pallas_call x1, Pallas kernels: 43.3 us -> 46.2 us  [per_device(): pl.pallas_call(functools.partial(kernel, (group, groups, parts, frames, w...]
    unnamed x13 -> x1, local copies, waits for them, and re-layouts: 4.72 us -> 1.97 us
    convert_element_type x3 -> x0, other arithmetic: 1.32 us -> none  [the longest x1 0.66 us: rope_tables(): pos_t.astype(jnp.float32)[:, None, None, None] * freq_time]
where the time goes in v1:
time: 49 us; the launch traced here: 48.9 us
  Pallas kernels  46.2 us (94%)
  local copies, waits for them, and re-layouts  1.97 us (4%)
  between operations  0.66 us (1%)
    pallas_call x1, Pallas kernels, per_device(): pl.pallas_call(functools.partial(kernel, (group, groups, parts, frames, w...  46.2 us
    unnamed x1, local copies, waits for them, and re-layouts  1.97 us

profile of v1, /device:TPU:0, one launch (start us, length us, event | category | flops | bytes accessed | tf_op | source)
XLA Modules:
  0.0 48.9 jit_solution(14722391471194466659)
XLA Ops:
  0.7 46.2 %shard_map.91 = bf16[128,2560]{1,0:T(8,128)(2,1)} custom-call(bf16[4,1,32,2560]{3,2,1,0:T(8,128)(2,1)} %q_hbm.1, bf16[4,1,32,2560]{3,2,1,0:T(8,128)(2,1)} %k_hbm.1, bf16[4,1,32,2560]{3,2,1,0:T(8,128)(2,1)} %v_hbm.1, s32[4,1,4,27]{3,2,1,0:T(4,128)} %mask_hbm.1, s32[1,4]{1,0:T(1,128)} %bitcast.6, s32[1]{0:T(128)S(6)} %copy.12.pos_h_ref, s32[1,32]{1,0:T(1,128)} %bitcast.7, ...), custom_call_target="tpu_custom_call" | custom-call | tf_op jit(solution)/shard_map/pallas_call | solution.py:424
  46.9 2.0 %copy.13 = bf16[4,1,32,2560]{3,2,1,0:T(8,128)(2,1)} copy(bf16[4,1,32,2560]{3,2,1,0:T(8,128)(2,1)} %bitcast.5) | data formatting | bytes 1310720

commit v2 on v1

--- a/solution.py
+++ b/solution.py
@@ -286,9 +286,6 @@
     if heads > 1:
         make_rows(1)
         send_rows(1)
-    loads[6].wait()
-    make_queries(0)
-    send_queries(0)
     if heads > 2:
         make_rows(2)
         send_rows(2)
@@ -312,11 +309,12 @@
             send_rows(s + 3)
 
         def more_queries():
-            make_queries(s + 1)
-            send_queries(s + 1)
-
+            make_queries(s)
+            send_queries(s)
+
+        pl.when(s == 0)(loads[6].wait)
+        more_queries()
         pl.when(s + 3 < heads)(more_rows)
-        pl.when(s + 1 < heads)(more_queries)
 
         @pl.when(c == 0)
         def _():
@@ -337,14 +335,13 @@
 
     factor = math.log2(math.e) / math.sqrt(dim)
 
+    def pass_on(j):
+        for step in range(1, groups):
+            first_got(j, step).wait_recv()
+        for to in range(1, parts):
+            first_on(j, to).start()
+
     def attend(j):
-        @pl.when(c == 0)
-        def _():
-            for step in range(1, groups):
-                first_got(j, step).wait_recv()
-            for to in range(1, parts):
-                first_on(j, to).start()
-
         pl.when(c > 0)(lambda: first_on(j, 1).wait_recv())
         for n in range(len(NEAR)):
             pl.when(near_here(n, -1))(lambda n=n: near_copy(j, n).wait_recv())
@@ -355,20 +352,26 @@
         far_v = first[j, 1].reshape(-1, dim)
         far_v = jnp.concatenate([far_v, jnp.ones_like(far_v)], axis=1)
         last = (((1,), (1,)), ((), ()))
+        s_all = lax.dot_general(
+            q_all[j].reshape(frames * tokens, dim), far_k, last, preferred_element_type=jnp.float32
+        )
+        near, p_all = [], []
         for f in range(frames):
             q = q_all[j, f].reshape(tokens, dim)
             near_k = ext[j, 0, pl.ds(f, 3)].reshape(-1, dim)
             near_v = ext[j, 1, pl.ds(f, 3)].reshape(-1, dim)
             near_v = jnp.concatenate([near_v, jnp.ones_like(near_v)], axis=1)
             s_near = lax.dot_general(q, near_k, last, preferred_element_type=jnp.float32) + bias[f]
-            s_far = lax.dot_general(q, far_k, last, preferred_element_type=jnp.float32)
+            s_far = s_all[f * tokens : (f + 1) * tokens]
             top = jnp.maximum(
                 jnp.max(s_near, axis=1, keepdims=True), jnp.max(s_far, axis=1, keepdims=True)
             )
             p_near = jnp.exp2((s_near - top) * factor).astype(jnp.bfloat16)
-            p_far = jnp.exp2((s_far - top) * factor).astype(jnp.bfloat16)
-            both = jnp.dot(p_near, near_v, preferred_element_type=jnp.float32)
-            both = both + jnp.dot(p_far, far_v, preferred_element_type=jnp.float32)
+            p_all.append(jnp.exp2((s_far - top) * factor).astype(jnp.bfloat16))
+            near.append(jnp.dot(p_near, near_v, preferred_element_type=jnp.float32))
+        far = jnp.dot(jnp.concatenate(p_all, axis=0), far_v, preferred_element_type=jnp.float32)
+        for f in range(frames):
+            both = near[f] + far[f * tokens : (f + 1) * tokens]
             result = (both[:, :dim] / both[:, dim:]).astype(jnp.bfloat16)
             held[j, :, pl.ds(f * width, width)] = result.reshape(group, width, dim)
         for step in range(1, group):
@@ -378,10 +381,11 @@
     def turn(s, carry):
         pl.when(s < heads)(lambda: spread_on(s))
         pl.when(s == 0)(make_bias)
-        pl.when(s > 0)(lambda: attend(s - 1))
+        pl.when(s > 1)(lambda: attend(s - 2))
+        pl.when((c == 0) & (s > 0) & (s <= heads))(lambda: pass_on(s - 1))
         return carry
 
-    lax.fori_loop(0, heads + 1, turn, 0)
+    lax.fori_loop(0, heads + 2, turn, 0)
 
     def finish(j, carry):
         for step in range(1, group):
@@ -421,6 +425,7 @@
     const = np.pad(const, ((0, -len(const) % 8), (0, 0)))
     keys_near = pick.shape[2]
     sem = pltpu.SemaphoreType.DMA
+    in_hbm = functools.partial(pltpu.with_memory_space_constraint, memory_space=pltpu.HBM)
     out = pl.pallas_call(
         functools.partial(kernel, (group, groups, parts, frames, width, heads)),
         out_shape=jax.ShapeDtypeStruct((tokens, channels), jnp.bfloat16),
@@ -464,18 +469,15 @@
             sem((group,)),
         ],
         compiler_params=pltpu.CompilerParams(
-            collective_id=0, has_side_effects=True, vmem_limit_bytes=62 * 1024 * 1024
+            collective_id=0, has_side_effects=True, vmem_limit_bytes=48 * 1024 * 1024
         ),
     )(
-        queries,
-        keys,
-        values,
-        window_mask,
-        pos_t.reshape(1, -1),
+        *(in_hbm(x) for x in (queries, keys, values, window_mask)),
+        in_hbm(pos_t.reshape(1, -1)),
         pos_h,
-        pos_w.reshape(1, -1),
-        jnp.asarray(const),
-        jnp.asarray(pick, jnp.bfloat16),
+        in_hbm(pos_w.reshape(1, -1)),
+        in_hbm(jnp.asarray(const)),
+        in_hbm(jnp.asarray(pick, jnp.bfloat16)),
     )
     return out.reshape(queries.shape)
 

time: 49 us -> 43.7 us (0.89)
  Pallas kernels: 46.2 us -> 41.9 us
  local copies, waits for them, and re-layouts: 1.97 us -> 0.84 us
    pallas_call x1, Pallas kernels: 46.2 us -> 41.9 us  [per_device(): pl.pallas_call(functools.partial(kernel, (group, groups, parts, frames, w...]
    unnamed x1, local copies, waits for them, and re-layouts: 1.97 us -> 0.84 us
where the time goes in v2:
time: 43.7 us; the launch traced here: 43.4 us
  Pallas kernels  41.9 us (96%)
  local copies, waits for them, and re-layouts  0.84 us (2%)
  between operations  0.66 us (2%)
    pallas_call x1, Pallas kernels, per_device(): pl.pallas_call(functools.partial(kernel, (group, groups, parts, frames, w...  41.9 us

profile of v2, /device:TPU:0, one launch (start us, length us, event | category | flops | bytes accessed | tf_op | source)
XLA Modules:
  0.0 43.4 jit_solution(11130069911530469979)
XLA Ops:
  0.7 41.9 %shard_map.91 = bf16[128,2560]{1,0:T(8,128)(2,1)S(1)} custom-call(bf16[4,1,32,2560]{3,2,1,0:T(8,128)(2,1)} %q_hbm.1, bf16[4,1,32,2560]{3,2,1,0:T(8,128)(2,1)} %k_hbm.1, bf16[4,1,32,2560]{3,2,1,0:T(8,128)(2,1)} %v_hbm.1, s32[4,1,4,27]{3,2,1,0:T(4,128)} %mask_hbm.1, s32[1,4]{1,0:T(1,128)} %bitcast.6, s32[1]{0:T(128)S(6)} %copy.12.pos_h_ref, s32[1,32]{1,0:T(1,128)} %bitcast.7, ...), custom_call_target="tpu_custom_call" | custom-call | tf_op jit(solution)/shard_map/pallas_call | solution.py:429
  42.5 0.8 %copy.13 = bf16[4,1,32,2560]{3,2,1,0:T(8,128)(2,1)} copy(bf16[4,1,32,2560]{3,2,1,0:T(8,128)(2,1)S(1)} %bitcast.5) | data formatting | bytes 1310720

commit v3 on v2

--- a/solution.py
+++ b/solution.py
@@ -14,6 +14,8 @@
 TILE_W = 8
 MESH = pl.DeviceIdType.MESH
 NEAR = [(dc, dg) for dc in (-1, 0, 1) for dg in (-1, 0, 1) if (dc, dg) != (0, 0)]
+ROWS = [n for n, (dc, dg) in enumerate(NEAR) if dc == 0]
+CORNERS = [n for n, (dc, dg) in enumerate(NEAR) if dc != 0 and dg != 0]
 
 
 def frequencies(half_dim):
@@ -52,7 +54,7 @@
     sizes, q_hbm, k_hbm, v_hbm, mask_hbm, pos_t_hbm, pos_h_ref, pos_w_hbm, const_hbm, pick_hbm, out_ref,
     q_ref, k_ref, v_ref, mask_in, pos_t_ref, pos_w_ref, const_ref, pick_ref,
     cos_ref, sin_ref, mask_pad, mask_ref, q_rot, rot, q_all, ext, first, held, masks, bias,
-    load, q_send, q_recv, a_send, a_recv, n_send, n_recv, f_send, f_recv, t_send, t_recv, o_send, o_recv, m_send, m_recv,
+    load, kv_load, q_send, q_recv, a_send, a_recv, n_send, n_recv, f_send, f_recv, r_send, r_recv, t_send, t_recv, o_send, o_recv, m_send, m_recv,
 ):
     group, groups, parts, frames, width, heads = sizes
     dim = HEAD_DIM
@@ -93,43 +95,62 @@
         dc, dg = NEAR[n]
         src_t = {-1: pl.ds(1, 1), 0: pl.ds(1, frames), 1: pl.ds(frames, 1)}[dc]
         dst_t = {-1: pl.ds(frames + 1, 1), 0: pl.ds(1, frames), 1: pl.ds(0, 1)}[dc]
-        src_h = {-1: pl.ds(1, 1), 0: pl.ds(1, group), 1: pl.ds(group, 1)}[dg]
-        dst_h = {-1: pl.ds(group + 1, 1), 0: pl.ds(1, group), 1: pl.ds(0, 1)}[dg]
+        if n in CORNERS:
+            src_h = dst_h = pl.ds(0 if dg < 0 else group + 1, 1)
+        else:
+            src_h = {-1: pl.ds(1, 1), 0: pl.ds(1, group), 1: pl.ds(group, 1)}[dg]
+            dst_h = {-1: pl.ds(group + 1, 1), 0: pl.ds(1, group), 1: pl.ds(0, 1)}[dg]
         return pltpu.make_async_remote_copy(
             src_ref=ext.at[j, :, src_t, src_h],
             dst_ref=ext.at[j, :, dst_t, dst_h],
             send_sem=n_send.at[j, n],
             recv_sem=n_recv.at[j, n],
-            device_id=(c + dc, at + dg * group),
+            device_id=(c + dc, at if n in CORNERS else at + dg * group),
             device_id_type=MESH,
         )
 
     def near_here(n, sign):
-        dc, dg = sign * NEAR[n][0], sign * NEAR[n][1]
+        dc, dg = sign * NEAR[n][0], NEAR[n][1] if n in CORNERS else sign * NEAR[n][1]
         ok = (c + dc >= 0) & (c + dc < parts)
         return ok & (g + dg >= 0) & (g + dg < groups)
 
-    def first_copy(j, step):
-        to = (g + step) % groups
+    def first_copy(j, to, owner, n):
         return pltpu.make_async_remote_copy(
             src_ref=ext.at[j, :, 1, pl.ds(1, group)],
-            dst_ref=first.at[j, :, pl.ds(g * group, group)],
-            send_sem=f_send.at[j, step - 1],
-            recv_sem=f_recv.at[j, g],
+            dst_ref=first.at[j, :, pl.ds(owner * group, group)],
+            send_sem=f_send.at[j, n],
+            recv_sem=f_recv.at[j, owner],
             device_id=(c, to * group + m),
             device_id_type=MESH,
         )
 
-    def first_got(j, step):
-        come = (g + step) % groups
-        return pltpu.make_async_remote_copy(
-            src_ref=ext.at[j, :, 1, pl.ds(1, group)],
-            dst_ref=first.at[j, :, pl.ds(come * group, group)],
-            send_sem=f_send.at[j, step - 1],
-            recv_sem=f_recv.at[j, come],
-            device_id=(c, come * group + m),
-            device_id_type=MESH,
-        )
+    half = groups // 2 if groups % 2 == 0 and groups > 2 else groups
+    side = g // half
+    gate = (g == half) | (g == half - 1)
+
+    def beside(step):
+        return side * half + (g % half + step) % half
+
+    def first_targets():
+        own_half = [beside(step) for step in range(1, half)]
+        return own_half + ([half - side] if half < groups else [])
+
+    def hand_copy(j, step):
+        rows = pl.ds((1 - side) * half * group, half * group)
+        return pltpu.make_async_remote_copy(
+            src_ref=first.at[j, :, rows],
+            dst_ref=first.at[j, :, rows],
+            send_sem=r_send.at[j, step - 1],
+            recv_sem=r_recv.at[j],
+            device_id=(c, beside(step) * group + m),
+            device_id_type=MESH,
+        )
+
+    def hand_on(j):
+        for n in range(half):
+            first_copy(j, (1 - side) * half + n, (1 - side) * half + n, 0).wait_recv()
+        for step in range(1, half):
+            hand_copy(j, step).start()
 
     def first_on(j, to):
         return pltpu.make_async_remote_copy(
@@ -232,11 +253,19 @@
         for n, (src, dst) in enumerate(
             [
                 (const_hbm, const_ref), (pos_t_hbm, pos_t_ref), (pos_w_hbm, pos_w_ref),
-                (mask_hbm, mask_in), (k_hbm, k_ref), (v_hbm, v_ref), (q_hbm, q_ref), (pick_hbm, pick_ref),
+                (mask_hbm, mask_in), (q_hbm, q_ref), (pick_hbm, pick_ref),
             ]
         )
     ]
-    for copy in loads:
+    def row_load(part, kind, p):
+        cols = pl.ds(p * heads * dim, dim) if part == 0 else pl.ds((p * heads + 1) * dim, (heads - 1) * dim)
+        src, dst = ((k_hbm, k_ref), (v_hbm, v_ref))[kind]
+        return pltpu.make_async_copy(src.at[:, :, :, cols], dst.at[:, :, :, cols], kv_load.at[part, kind, p])
+
+    row_loads = [
+        [row_load(part, kind, p) for kind in range(2) for p in range(group)] for part in range(2 if heads > 1 else 1)
+    ]
+    for copy in loads[:4] + row_loads[0] + sum(row_loads[1:], []) + loads[4:]:
         copy.start()
 
     pl.when(c == 0)(lambda: clear(ext.at[:, :, 0]))
@@ -278,12 +307,14 @@
         mask_ref[f : f + 1, :] = line
     masks[m] = mask_ref[...]
 
-    loads[4].wait()
-    loads[5].wait()
+    for copy in row_loads[0]:
+        copy.wait()
     make_rows(0)
     pl.semaphore_wait(barrier, group - 1 + parts * groups - 1)
     send_rows(0)
     if heads > 1:
+        for copy in row_loads[1]:
+            copy.wait()
         make_rows(1)
         send_rows(1)
     if heads > 2:
@@ -298,11 +329,12 @@
 
         @pl.when(c == 0)
         def _():
-            for step in range(1, groups):
-                first_copy(s, step).start()
+            for n, to in enumerate(first_targets()):
+                first_copy(s, to, g, n).start()
 
         for n in range(len(NEAR)):
-            pl.when(near_here(n, 1))(lambda n=n: near_copy(s, n).start())
+            if n not in CORNERS:
+                pl.when(near_here(n, 1))(lambda n=n: near_copy(s, n).start())
 
         def more_rows():
             make_rows(s + 3)
@@ -312,7 +344,7 @@
             make_queries(s)
             send_queries(s)
 
-        pl.when(s == 0)(loads[6].wait)
+        pl.when(s == 0)(loads[4].wait)
         more_queries()
         pl.when(s + 3 < heads)(more_rows)
 
@@ -323,7 +355,7 @@
     def make_bias():
         for step in range(1, group):
             mask_got(step).wait_recv()
-        loads[7].wait()
+        loads[5].wait()
         for row in range(group):
             spread = jnp.concatenate(
                 [jnp.broadcast_to(masks[row, f : f + 1, :], (width, masks.shape[2])) * const_ref[0:width, :] for f in range(frames)],
@@ -336,15 +368,24 @@
     factor = math.log2(math.e) / math.sqrt(dim)
 
     def pass_on(j):
-        for step in range(1, groups):
-            first_got(j, step).wait_recv()
+        for step in range(1, half):
+            first_copy(j, beside(step), beside(step), 0).wait_recv()
+        if half < groups:
+            pl.when(jnp.logical_not(gate))(lambda: hand_copy(j, 1).wait_recv())
         for to in range(1, parts):
             first_on(j, to).start()
+
+    def send_corners(j):
+        for n in ROWS:
+            pl.when(near_here(n, -1))(lambda n=n: near_copy(j, n).wait_recv())
+        for n in CORNERS:
+            pl.when(near_here(n, 1))(lambda n=n: near_copy(j, n).start())
 
     def attend(j):
         pl.when(c > 0)(lambda: first_on(j, 1).wait_recv())
         for n in range(len(NEAR)):
-            pl.when(near_here(n, -1))(lambda n=n: near_copy(j, n).wait_recv())
+            if n not in ROWS:
+                pl.when(near_here(n, -1))(lambda n=n: near_copy(j, n).wait_recv())
 
         for step in range(1, group):
             query_copy(j, step, True).wait_recv()
@@ -381,7 +422,10 @@
     def turn(s, carry):
         pl.when(s < heads)(lambda: spread_on(s))
         pl.when(s == 0)(make_bias)
+        if half < groups:
+            pl.when((c == 0) & gate & (s > 0) & (s <= heads))(lambda: hand_on(s - 1))
         pl.when(s > 1)(lambda: attend(s - 2))
+        pl.when((s > 0) & (s <= heads))(lambda: send_corners(s - 1))
         pl.when((c == 0) & (s > 0) & (s <= heads))(lambda: pass_on(s - 1))
         return carry
 
@@ -398,10 +442,17 @@
 
         @pl.when(c == 0)
         def _():
-            for step in range(1, groups):
-                first_copy(j, step).wait_send()
+            for n, to in enumerate(first_targets()):
+                first_copy(j, to, g, n).wait_send()
             for to in range(1, parts):
                 first_on(j, to).wait_send()
+
+        if half < groups:
+
+            @pl.when((c == 0) & gate)
+            def _():
+                for step in range(1, half):
+                    hand_copy(j, step).wait_send()
 
         return carry
 
@@ -452,7 +503,8 @@
             pltpu.VMEM((heads, group, tokens, dim), jnp.bfloat16),
             pltpu.VMEM((group, mask_rows, lanes), jnp.float32),
             pltpu.VMEM((frames, group * width, keys_near), jnp.float32),
-            sem((8,)),
+            sem((6,)),
+            sem((2, 2, group)),
             sem((heads, max(1, group - 1))),
             sem((heads, group)),
             sem((heads, max(1, group - 1))),
@@ -461,6 +513,8 @@
             sem((heads, len(NEAR))),
             sem((heads, max(1, groups - 1))),
             sem((heads, groups)),
+            sem((heads, max(1, groups - 1))),
+            sem((heads,)),
             sem((heads, max(1, parts - 1))),
             sem((heads,)),
             sem((heads, max(1, group - 1))),

time: 43.7 us -> 48.5 us (1.11)
  Pallas kernels: 41.9 us -> 46.6 us
    pallas_call x1, Pallas kernels: 41.9 us -> 46.6 us  [per_device(): pl.pallas_call(functools.partial(kernel, (group, groups, parts, frames, w...]
where the time goes in v3:
time: 48.5 us; the launch traced here: 48.1 us
  Pallas kernels  46.6 us (96%)
  local copies, waits for them, and re-layouts  0.84 us (2%)
  between operations  0.66 us (1%)
    pallas_call x1, Pallas kernels, per_device(): pl.pallas_call(functools.partial(kernel, (group, groups, parts, frames, w...  46.6 us

profile of v3, /device:TPU:0, one launch (start us, length us, event | category | flops | bytes accessed | tf_op | source)
XLA Modules:
  0.0 48.1 jit_solution(10488852739477363455)
XLA Ops:
  0.7 46.6 %shard_map.91 = bf16[128,2560]{1,0:T(8,128)(2,1)S(1)} custom-call(bf16[4,1,32,2560]{3,2,1,0:T(8,128)(2,1)} %q_hbm.1, bf16[4,1,32,2560]{3,2,1,0:T(8,128)(2,1)} %k_hbm.1, bf16[4,1,32,2560]{3,2,1,0:T(8,128)(2,1)} %v_hbm.1, s32[4,1,4,27]{3,2,1,0:T(4,128)} %mask_hbm.1, s32[1,4]{1,0:T(1,128)} %bitcast.6, s32[1]{0:T(128)S(6)} %copy.12.pos_h_ref, s32[1,32]{1,0:T(1,128)} %bitcast.7, ...), custom_call_target="tpu_custom_call" | custom-call | tf_op jit(solution)/shard_map/pallas_call | solution.py:480
  47.3 0.8 %copy.13 = bf16[4,1,32,2560]{3,2,1,0:T(8,128)(2,1)} copy(bf16[4,1,32,2560]{3,2,1,0:T(8,128)(2,1)S(1)} %bitcast.5) | data formatting | bytes 1310720

commit v4 on v2

--- a/solution.py
+++ b/solution.py
@@ -52,7 +52,7 @@
     sizes, q_hbm, k_hbm, v_hbm, mask_hbm, pos_t_hbm, pos_h_ref, pos_w_hbm, const_hbm, pick_hbm, out_ref,
     q_ref, k_ref, v_ref, mask_in, pos_t_ref, pos_w_ref, const_ref, pick_ref,
     cos_ref, sin_ref, mask_pad, mask_ref, q_rot, rot, q_all, ext, first, held, masks, bias,
-    load, q_send, q_recv, a_send, a_recv, n_send, n_recv, f_send, f_recv, t_send, t_recv, o_send, o_recv, m_send, m_recv,
+    load, kv_load, q_send, q_recv, a_send, a_recv, n_send, n_recv, f_send, f_recv, t_send, t_recv, o_send, o_recv, m_send, m_recv,
 ):
     group, groups, parts, frames, width, heads = sizes
     dim = HEAD_DIM
@@ -205,6 +205,10 @@
         for step in range(1, group):
             row_copy(j, step, False).start()
 
+    def rows_left(j):
+        for step in range(1, group):
+            row_copy(j, step, False).wait_send()
+
     def make_queries(j):
         for step in range(1, group):
             head = peer(step) * heads + j
@@ -232,11 +236,19 @@
         for n, (src, dst) in enumerate(
             [
                 (const_hbm, const_ref), (pos_t_hbm, pos_t_ref), (pos_w_hbm, pos_w_ref),
-                (mask_hbm, mask_in), (k_hbm, k_ref), (v_hbm, v_ref), (q_hbm, q_ref), (pick_hbm, pick_ref),
+                (mask_hbm, mask_in), (q_hbm, q_ref), (pick_hbm, pick_ref),
             ]
         )
     ]
-    for copy in loads:
+    def row_load(part, kind, p):
+        cols = pl.ds(p * heads * dim, dim) if part == 0 else pl.ds((p * heads + 1) * dim, (heads - 1) * dim)
+        src, dst = ((k_hbm, k_ref), (v_hbm, v_ref))[kind]
+        return pltpu.make_async_copy(src.at[:, :, :, cols], dst.at[:, :, :, cols], kv_load.at[part, kind, p])
+
+    row_loads = [
+        [row_load(part, kind, p) for kind in range(2) for p in range(group)] for part in range(2 if heads > 1 else 1)
+    ]
+    for copy in loads[:4] + row_loads[0] + sum(row_loads[1:], []) + loads[4:]:
         copy.start()
 
     pl.when(c == 0)(lambda: clear(ext.at[:, :, 0]))
@@ -278,17 +290,17 @@
         mask_ref[f : f + 1, :] = line
     masks[m] = mask_ref[...]
 
-    loads[4].wait()
-    loads[5].wait()
+    for copy in row_loads[0]:
+        copy.wait()
     make_rows(0)
     pl.semaphore_wait(barrier, group - 1 + parts * groups - 1)
     send_rows(0)
     if heads > 1:
+        for copy in row_loads[1]:
+            copy.wait()
         make_rows(1)
+        rows_left(0)
         send_rows(1)
-    if heads > 2:
-        make_rows(2)
-        send_rows(2)
     for step in range(1, group):
         mask_copy(step).start()
 
@@ -305,16 +317,17 @@
             pl.when(near_here(n, 1))(lambda n=n: near_copy(s, n).start())
 
         def more_rows():
-            make_rows(s + 3)
-            send_rows(s + 3)
+            make_rows(s + 2)
+            rows_left(s + 1)
+            send_rows(s + 2)
 
         def more_queries():
             make_queries(s)
             send_queries(s)
 
-        pl.when(s == 0)(loads[6].wait)
+        pl.when(s == 0)(loads[4].wait)
+        pl.when(s + 2 < heads)(more_rows)
         more_queries()
-        pl.when(s + 3 < heads)(more_rows)
 
         @pl.when(c == 0)
         def _():
@@ -323,7 +336,7 @@
     def make_bias():
         for step in range(1, group):
             mask_got(step).wait_recv()
-        loads[7].wait()
+        loads[5].wait()
         for row in range(group):
             spread = jnp.concatenate(
                 [jnp.broadcast_to(masks[row, f : f + 1, :], (width, masks.shape[2])) * const_ref[0:width, :] for f in range(frames)],
@@ -387,9 +400,10 @@
 
     lax.fori_loop(0, heads + 2, turn, 0)
 
+    rows_left(heads - 1)
+
     def finish(j, carry):
         for step in range(1, group):
-            row_copy(j, step, False).wait_send()
             query_copy(j, step, False).wait_send()
             out_copy(j, step).wait_send()
             out_got(j, step).wait_recv()
@@ -452,7 +466,8 @@
             pltpu.VMEM((heads, group, tokens, dim), jnp.bfloat16),
             pltpu.VMEM((group, mask_rows, lanes), jnp.float32),
             pltpu.VMEM((frames, group * width, keys_near), jnp.float32),
-            sem((8,)),
+            sem((6,)),
+            sem((2, 2, group)),
             sem((heads, max(1, group - 1))),
             sem((heads, group)),
             sem((heads, max(1, group - 1))),

time: 43.7 us -> 42.5 us (0.973)
  Pallas kernels: 41.9 us -> 40.7 us
    pallas_call x1, Pallas kernels: 41.9 us -> 40.7 us  [per_device(): pl.pallas_call(functools.partial(kernel, (group, groups, parts, frames, w...]
where the time goes in v4:
time: 42.5 us; the launch traced here: 42.2 us
  Pallas kernels  40.7 us (96%)
  local copies, waits for them, and re-layouts  0.84 us (2%)
  between operations  0.66 us (2%)
    pallas_call x1, Pallas kernels, per_device(): pl.pallas_call(functools.partial(kernel, (group, groups, parts, frames, w...  40.7 us

profile of v4, /device:TPU:0, one launch (start us, length us, event | category | flops | bytes accessed | tf_op | source)
XLA Modules:
  0.0 42.2 jit_solution(2854746558782314894)
XLA Ops:
  0.7 40.7 %shard_map.91 = bf16[128,2560]{1,0:T(8,128)(2,1)S(1)} custom-call(bf16[4,1,32,2560]{3,2,1,0:T(8,128)(2,1)} %q_hbm.1, bf16[4,1,32,2560]{3,2,1,0:T(8,128)(2,1)} %k_hbm.1, bf16[4,1,32,2560]{3,2,1,0:T(8,128)(2,1)} %v_hbm.1, s32[4,1,4,27]{3,2,1,0:T(4,128)} %mask_hbm.1, s32[1,4]{1,0:T(1,128)} %bitcast.6, s32[1]{0:T(128)S(6)} %copy.12.pos_h_ref, s32[1,32]{1,0:T(1,128)} %bitcast.7, ...), custom_call_target="tpu_custom_call" | custom-call | tf_op jit(solution)/shard_map/pallas_call | solution.py:443
  41.4 0.8 %copy.13 = bf16[4,1,32,2560]{3,2,1,0:T(8,128)(2,1)} copy(bf16[4,1,32,2560]{3,2,1,0:T(8,128)(2,1)S(1)} %bitcast.5) | data formatting | bytes 1310720

commit v5 on v4

--- a/solution.py
+++ b/solution.py
@@ -251,13 +251,7 @@
     for copy in loads[:4] + row_loads[0] + sum(row_loads[1:], []) + loads[4:]:
         copy.start()
 
-    pl.when(c == 0)(lambda: clear(ext.at[:, :, 0]))
-    pl.when(c == parts - 1)(lambda: clear(ext.at[:, :, frames + 1]))
-    pl.when(g == 0)(lambda: clear(ext.at[:, :, :, 0]))
-    pl.when(g == groups - 1)(lambda: clear(ext.at[:, :, :, group + 1]))
-    clear(mask_pad)
-
-    for copy in loads[:4]:
+    for copy in loads[:3]:
         copy.wait()
 
     def column(ref, rows):
@@ -278,6 +272,19 @@
         for f in range(frames):
             part = jnp.where(freq_t > 0, of_t[f : f + 1, :], of_hw)
             table[pl.ds(f * width, width), :] = part if factor is None else part * factor
+    for copy in row_loads[0]:
+        copy.wait()
+    make_rows(0)
+    pl.semaphore_wait(barrier, group - 1 + parts * groups - 1)
+    send_rows(0)
+
+    pl.when(c == 0)(lambda: clear(ext.at[:, :, 0]))
+    pl.when(c == parts - 1)(lambda: clear(ext.at[:, :, frames + 1]))
+    pl.when(g == 0)(lambda: clear(ext.at[:, :, :, 0]))
+    pl.when(g == groups - 1)(lambda: clear(ext.at[:, :, :, group + 1]))
+    clear(mask_pad)
+
+    loads[3].wait()
     slot = mask_ref.shape[1] // mask_in.shape[2]
     for f in range(frames):
         mask_pad[f, pl.ds(0, mask_in.shape[2]), pl.ds(0, mask_in.shape[3])] = (mask_in[f, 0] > 0).astype(jnp.float32)
@@ -290,11 +297,6 @@
         mask_ref[f : f + 1, :] = line
     masks[m] = mask_ref[...]
 
-    for copy in row_loads[0]:
-        copy.wait()
-    make_rows(0)
-    pl.semaphore_wait(barrier, group - 1 + parts * groups - 1)
-    send_rows(0)
     if heads > 1:
         for copy in row_loads[1]:
             copy.wait()
@@ -394,8 +396,9 @@
     def turn(s, carry):
         pl.when(s < heads)(lambda: spread_on(s))
         pl.when(s == 0)(make_bias)
+        pl.when((c == 0) & (s == heads))(lambda: pass_on(s - 1))
         pl.when(s > 1)(lambda: attend(s - 2))
-        pl.when((c == 0) & (s > 0) & (s <= heads))(lambda: pass_on(s - 1))
+        pl.when((c == 0) & (s > 0) & (s < heads))(lambda: pass_on(s - 1))
         return carry
 
     lax.fori_loop(0, heads + 2, turn, 0)

time: 42.5 us -> 43.9 us (1.033)
  Pallas kernels: 40.7 us -> 42.2 us
    pallas_call x1, Pallas kernels: 40.7 us -> 42.2 us  [per_device(): pl.pallas_call(functools.partial(kernel, (group, groups, parts, frames, w...]
where the time goes in v5:
time: 43.9 us; the launch traced here: 43.7 us
  Pallas kernels  42.2 us (96%)
  local copies, waits for them, and re-layouts  0.84 us (2%)
  between operations  0.66 us (2%)
    pallas_call x1, Pallas kernels, per_device(): pl.pallas_call(functools.partial(kernel, (group, groups, parts, frames, w...  42.2 us

profile of v5, /device:TPU:0, one launch (start us, length us, event | category | flops | bytes accessed | tf_op | source)
XLA Modules:
  0.0 43.7 jit_solution(1881389184913850628)
XLA Ops:
  0.7 42.2 %shard_map.91 = bf16[128,2560]{1,0:T(8,128)(2,1)S(1)} custom-call(bf16[4,1,32,2560]{3,2,1,0:T(8,128)(2,1)} %q_hbm.1, bf16[4,1,32,2560]{3,2,1,0:T(8,128)(2,1)} %k_hbm.1, bf16[4,1,32,2560]{3,2,1,0:T(8,128)(2,1)} %v_hbm.1, s32[4,1,4,27]{3,2,1,0:T(4,128)} %mask_hbm.1, s32[1,4]{1,0:T(1,128)} %bitcast.6, s32[1]{0:T(128)S(6)} %copy.12.pos_h_ref, s32[1,32]{1,0:T(1,128)} %bitcast.7, ...), custom_call_target="tpu_custom_call" | custom-call | tf_op jit(solution)/shard_map/pallas_call | solution.py:446
  42.9 0.8 %copy.13 = bf16[4,1,32,2560]{3,2,1,0:T(8,128)(2,1)} copy(bf16[4,1,32,2560]{3,2,1,0:T(8,128)(2,1)S(1)} %bitcast.5) | data formatting | bytes 1310720
